TPU v7x, 256 devices: a whole 4x4x8 slice. The times are simulated.
256 devices in a mesh: rank: 4 (over x_lo, core), basis: 64 (over y, x_hi, z).
Axes of the slice: x: 4 (x_hi: 2, x_lo: 2; x = x_hi * 2 + x_lo), y: 4, z: 8, core: 2. Of those that a mesh axis runs over, the one named last changes fastest.
Arguments:
- factors: bfloat16 [4, 16384, 1024], P('rank', 'basis'), may hold values from -0.796875 to 0.796875
Outputs:
- exchange_matrix: float32 [16384, 16384], P('basis', 'rank')
All inputs are finite; a program needn't handle non-finite values.
Results may differ from a plain program's by a relative error of at most 0.012.
Values may be sent and summed in bfloat16 or wider, within the bound.
A program may use at most 128 MiB of HBM per device.

v0:
```python
import jax
import jax.numpy as jnp
from jax import lax
from jax.sharding import PartitionSpec as P


def passed_along(value, axis, steps):
    count = lax.axis_size(axis)
    pairs = [(source, (source + steps) % count) for source in range(count)]
    return lax.ppermute(value, axis, pairs)


def pair_tile(left, right):
    return jnp.einsum("qmi,qni->mn", left, right, preferred_element_type=jnp.float32)


def to_absolute(buffer, count, me):
    doubled = jnp.concatenate([buffer, buffer], axis=0)
    return lax.dynamic_slice_in_dim(doubled, count - me, count, 0)


def weights_for(step, half, me):
    lower_side = me < half
    middle = step == half
    keep_own = jnp.where(jnp.logical_and(middle, jnp.logical_not(lower_side)), 0.0, 1.0).astype(
        jnp.float32
    )
    keep_out = jnp.where(
        jnp.logical_or(step < half, jnp.logical_and(middle, lower_side)), 1.0, 0.0
    ).astype(jnp.float32)
    return (keep_own, keep_out)


def local(factors):
    count = lax.axis_size("basis")
    half = count // 2
    rows = factors.shape[1]
    me = lax.axis_index("basis")
    own_tiles = jnp.zeros((count, rows, rows), jnp.float32)
    own_tiles = own_tiles.at[0].set(pair_tile(factors, factors))
    outgoing = jnp.zeros((count, rows, rows), jnp.float32)

    def advance(step, carry):
        moving, own_now, out_now = carry
        moving = passed_along(moving, "basis", -1)
        part = pair_tile(factors, moving)
        keep_own, keep_out = weights_for(step, half, me)
        own_now = own_now.at[step].add(part * keep_own)
        out_now = out_now.at[step].add(part.T * keep_out)
        return (moving, own_now, out_now)

    carry = lax.fori_loop(1, half + 1, advance, (factors, own_tiles, outgoing))
    own_tiles, outgoing = (carry[1], carry[2])
    own_abs = to_absolute(own_tiles, count, me)
    out_abs = to_absolute(outgoing, count, me).astype(jnp.bfloat16)
    received = lax.all_to_all(out_abs, "basis", split_axis=0, concat_axis=0, tiled=True)
    row_tiles = own_abs + received.astype(jnp.float32)
    row_block = jnp.transpose(row_tiles, (1, 0, 2)).reshape(rows, count * rows)
    return lax.psum_scatter(
        row_block.astype(jnp.bfloat16), "rank", scatter_dimension=1, tiled=True
    ).astype(jnp.float32)


def solution(mesh):
    placed = (P("rank", "basis", None),)
    return jax.shard_map(
        local, mesh=mesh, in_specs=placed, out_specs=P("basis", "rank"), check_vma=False
    )
```

profile of v0, /device:TPU:1, one launch (start us, length us, event | category | flops | bytes accessed | tf_op | source)
XLA Modules:
  0.0 997.2 jit_solution(17176160506088520668)
XLA Ops:
  9.2 7.8 scatter.4.clone
  17.0 7.8 broadcast.91
  24.8 657.7 %while.24 = (s32[]{:T(128)}, bf16[1,256,1024]{2,1,0:T(8,128)(2,1)S(1)}, f32[64,256,256]{1,2,0:T(8,128)}, f32[64,256,256]{1,2,0:T(8,128)}, bf16[1,256,1024]{2,1,0...) while((s32[]{:T(128)}, ...), condition=%wide.region_2.0_spmd, body=%wide.region_0.2_spmd.sunk | while | flops 134610976 | bytes 6293809 | solution.py:52
  24.8 11.3 %collective-permute-start = (bf16[1,256,1024]{2,1,0:T(8,128)(2,1)S(1)}, bf16[1,256,1024]{2,1,0:T(8,128)(2,1)S(1)}, u32[]{:S(2)}, u32[]{:S(2)}) collective-permute-start(bf16[1,256,1024]{2,1,0:T(8,128)(2,1)S(1)} %get-tuple-element.356), channel_id=1, source_target_pairs={{0,63},{1,0},{2,1},{3,2},{4,3},{5,4},{6,5},{7,6},{8,7},{9,8},{10,9... | collective-permute-start | bytes 1572872 | tf_op jit(solution)/shard_map/while/body/eval_jaxpr/ppermute | solution.py:10
  36.8 9.9 collective-permute-done
  51.8 8.0 collective-permute-start
  60.5 8.9 collective-permute-done
  74.6 8.0 collective-permute-start
  83.3 8.0 collective-permute-done
  96.4 8.0 collective-permute-start
  117.3 8.0 collective-permute-start
  137.4 8.0 collective-permute-start
  175.6 7.7 collective-permute-start
  213.4 7.7 collective-permute-start
  337.4 8.0 collective-permute-done
  359.0 9.1 collective-permute-done
  381.6 10.1 %collective-permute-done = bf16[1,256,1024]{2,1,0:T(8,128)(2,1)S(1)} collective-permute-done((bf16[1,256,1024]{2,1,0:T(8,128)(2,1)S(1)}, bf16[1,256,1024]{2,1,0:T(8,128)(2,1)S(1)}, u32[]{:S(2)}, u32[]{:S(2)}) %collective-permute-start) | collective-permute-done | bytes 524320 | tf_op jit(solution)/shard_map/while/body/eval_jaxpr/ppermute | solution.py:10
  396.9 7.7 collective-permute-start
  405.3 10.7 %collective-permute-done = bf16[1,256,1024]{2,1,0:T(8,128)(2,1)S(1)} collective-permute-done((bf16[1,256,1024]{2,1,0:T(8,128)(2,1)S(1)}, bf16[1,256,1024]{2,1,0:T(8,128)(2,1)S(1)}, u32[]{:S(2)}, u32[]{:S(2)}) %collective-permute-start) | collective-permute-done | bytes 524320 | tf_op jit(solution)/shard_map/while/body/eval_jaxpr/ppermute | solution.py:10
  421.2 8.0 collective-permute-start
  429.9 9.8 collective-permute-done
  444.9 8.0 collective-permute-start
  453.6 9.0 collective-permute-done
  467.7 8.0 collective-permute-start
  476.4 8.0 collective-permute-done
  489.6 8.0 collective-permute-start
  510.5 8.0 collective-permute-start
  530.5 8.0 collective-permute-start
  682.5 10.4 %fusion.6 = bf16[64,256,256]{1,2,0:T(8,128)(2,1)} fusion(s32[]{:T(128)S(6)} %select_n.44, f32[64,256,256]{1,2,0:T(8,128)} %get-tuple-element.269), kind=kLoop, calls=%fused_computation.13 | loop fusion | flops 4194304 | bytes 25165828 | tf_op jit(solution)/shard_map/convert_element_type | solution.py:55
  692.9 155.3 %all_to_all.5 = bf16[64,256,256]{1,2,0:T(8,128)(2,1)S(1)} all-to-all(bf16[64,256,256]{1,2,0:T(8,128)(2,1)} %fusion.6), channel_id=1, replica_groups=mesh['rank'=4,'basis'=64] {'basis'}, dimensions={0} | all-to-all | bytes 16777216 | tf_op jit(solution)/shard_map/all_to_all | solution.py:56
  854.5 11.9 %copy.5 = bf16[256,16384]{1,0:T(8,128)(2,1)} copy(bf16[256,16384]{0,1:T(8,128)(2,1)} %bitcast.38) | data formatting | bytes 16777216 | tf_op jit(solution)/shard_map/convert_element_type | solution.py:60
  866.4 119.8 %reduce-scatter.2.cloned.1.call-done = bf16[256,4096]{1,0:T(8,128)(2,1)} async-done(((bf16[256,16384]{1,0:T(8,128)(2,1)}), bf16[256,4096]{1,0:T(8,128)(2,1)}) %reduce-scatter.2.cloned.1.call-update) | async-done | bytes 2097168 | tf_op jit(solution)/shard_map/reduce_scatter | solution.py:59
  (218 shorter events, 455.8 us)
Async XLA Ops:
  6.5 979.7 %reduce-scatter.2.cloned.1.call-start = ((), (), s32[]{:S(2)}) async-start(), calls=%async_computation.2 | async-start | bytes 10485760 | tf_op jit(solution)/shard_map/reduce_scatter | solution.py:59
  24.8 21.9 %collective-permute-start = (bf16[1,256,1024]{2,1,0:T(8,128)(2,1)S(1)}, bf16[1,256,1024]{2,1,0:T(8,128)(2,1)S(1)}, u32[]{:S(2)}, u32[]{:S(2)}) collective-permute-start(bf16[1,256,1024]{2,1,0:T(8,128)(2,1)S(1)} %get-tuple-element.356), channel_id=1, source_target_pairs={{0,63},{1,0},{2,1},{3,2},{4,3},{5,4},{6,5},{7,6},{8,7},{9,8},{10,9... | collective-permute-start | bytes 1572872 | tf_op jit(solution)/shard_map/while/body/eval_jaxpr/ppermute | solution.py:10
  51.8 17.7 %collective-permute-start = (bf16[1,256,1024]{2,1,0:T(8,128)(2,1)S(1)}, bf16[1,256,1024]{2,1,0:T(8,128)(2,1)S(1)}, u32[]{:S(2)}, u32[]{:S(2)}) collective-permute-start(bf16[1,256,1024]{2,1,0:T(8,128)(2,1)S(1)} %get-tuple-element.356), channel_id=1, source_target_pairs={{0,63},{1,0},{2,1},{3,2},{4,3},{5,4},{6,5},{7,6},{8,7},{9,8},{10,9... | collective-permute-start | bytes 1572872 | tf_op jit(solution)/shard_map/while/body/eval_jaxpr/ppermute | solution.py:10
  74.6 16.7 %collective-permute-start = (bf16[1,256,1024]{2,1,0:T(8,128)(2,1)S(1)}, bf16[1,256,1024]{2,1,0:T(8,128)(2,1)S(1)}, u32[]{:S(2)}, u32[]{:S(2)}) collective-permute-start(bf16[1,256,1024]{2,1,0:T(8,128)(2,1)S(1)} %get-tuple-element.356), channel_id=1, source_target_pairs={{0,63},{1,0},{2,1},{3,2},{4,3},{5,4},{6,5},{7,6},{8,7},{9,8},{10,9... | collective-permute-start | bytes 1572872 | tf_op jit(solution)/shard_map/while/body/eval_jaxpr/ppermute | solution.py:10
  96.4 15.8 %collective-permute-start = (bf16[1,256,1024]{2,1,0:T(8,128)(2,1)S(1)}, bf16[1,256,1024]{2,1,0:T(8,128)(2,1)S(1)}, u32[]{:S(2)}, u32[]{:S(2)}) collective-permute-start(bf16[1,256,1024]{2,1,0:T(8,128)(2,1)S(1)} %get-tuple-element.356), channel_id=1, source_target_pairs={{0,63},{1,0},{2,1},{3,2},{4,3},{5,4},{6,5},{7,6},{8,7},{9,8},{10,9... | collective-permute-start | bytes 1572872 | tf_op jit(solution)/shard_map/while/body/eval_jaxpr/ppermute | solution.py:10
  117.3 14.9 %collective-permute-start = (bf16[1,256,1024]{2,1,0:T(8,128)(2,1)S(1)}, bf16[1,256,1024]{2,1,0:T(8,128)(2,1)S(1)}, u32[]{:S(2)}, u32[]{:S(2)}) collective-permute-start(bf16[1,256,1024]{2,1,0:T(8,128)(2,1)S(1)} %get-tuple-element.356), channel_id=1, source_target_pairs={{0,63},{1,0},{2,1},{3,2},{4,3},{5,4},{6,5},{7,6},{8,7},{9,8},{10,9... | collective-permute-start | bytes 1572872 | tf_op jit(solution)/shard_map/while/body/eval_jaxpr/ppermute | solution.py:10
  137.4 14.1 %collective-permute-start = (bf16[1,256,1024]{2,1,0:T(8,128)(2,1)S(1)}, bf16[1,256,1024]{2,1,0:T(8,128)(2,1)S(1)}, u32[]{:S(2)}, u32[]{:S(2)}) collective-permute-start(bf16[1,256,1024]{2,1,0:T(8,128)(2,1)S(1)} %get-tuple-element.356), channel_id=1, source_target_pairs={{0,63},{1,0},{2,1},{3,2},{4,3},{5,4},{6,5},{7,6},{8,7},{9,8},{10,9... | collective-permute-start | bytes 1572872 | tf_op jit(solution)/shard_map/while/body/eval_jaxpr/ppermute | solution.py:10
  156.6 13.8 %collective-permute-start = (bf16[1,256,1024]{2,1,0:T(8,128)(2,1)S(1)}, bf16[1,256,1024]{2,1,0:T(8,128)(2,1)S(1)}, u32[]{:S(2)}, u32[]{:S(2)}) collective-permute-start(bf16[1,256,1024]{2,1,0:T(8,128)(2,1)S(1)} %get-tuple-element.356), channel_id=1, source_target_pairs={{0,63},{1,0},{2,1},{3,2},{4,3},{5,4},{6,5},{7,6},{8,7},{9,8},{10,9... | collective-permute-start | bytes 1572872 | tf_op jit(solution)/shard_map/while/body/eval_jaxpr/ppermute | solution.py:10
  175.6 13.8 %collective-permute-start = (bf16[1,256,1024]{2,1,0:T(8,128)(2,1)S(1)}, bf16[1,256,1024]{2,1,0:T(8,128)(2,1)S(1)}, u32[]{:S(2)}, u32[]{:S(2)}) collective-permute-start(bf16[1,256,1024]{2,1,0:T(8,128)(2,1)S(1)} %get-tuple-element.356), channel_id=1, source_target_pairs={{0,63},{1,0},{2,1},{3,2},{4,3},{5,4},{6,5},{7,6},{8,7},{9,8},{10,9... | collective-permute-start | bytes 1572872 | tf_op jit(solution)/shard_map/while/body/eval_jaxpr/ppermute | solution.py:10
  194.5 13.8 %collective-permute-start = (bf16[1,256,1024]{2,1,0:T(8,128)(2,1)S(1)}, bf16[1,256,1024]{2,1,0:T(8,128)(2,1)S(1)}, u32[]{:S(2)}, u32[]{:S(2)}) collective-permute-start(bf16[1,256,1024]{2,1,0:T(8,128)(2,1)S(1)} %get-tuple-element.356), channel_id=1, source_target_pairs={{0,63},{1,0},{2,1},{3,2},{4,3},{5,4},{6,5},{7,6},{8,7},{9,8},{10,9... | collective-permute-start | bytes 1572872 | tf_op jit(solution)/shard_map/while/body/eval_jaxpr/ppermute | solution.py:10
  213.4 13.8 %collective-permute-start = (bf16[1,256,1024]{2,1,0:T(8,128)(2,1)S(1)}, bf16[1,256,1024]{2,1,0:T(8,128)(2,1)S(1)}, u32[]{:S(2)}, u32[]{:S(2)}) collective-permute-start(bf16[1,256,1024]{2,1,0:T(8,128)(2,1)S(1)} %get-tuple-element.356), channel_id=1, source_target_pairs={{0,63},{1,0},{2,1},{3,2},{4,3},{5,4},{6,5},{7,6},{8,7},{9,8},{10,9... | collective-permute-start | bytes 1572872 | tf_op jit(solution)/shard_map/while/body/eval_jaxpr/ppermute | solution.py:10
  232.4 13.8 %collective-permute-start = (bf16[1,256,1024]{2,1,0:T(8,128)(2,1)S(1)}, bf16[1,256,1024]{2,1,0:T(8,128)(2,1)S(1)}, u32[]{:S(2)}, u32[]{:S(2)}) collective-permute-start(bf16[1,256,1024]{2,1,0:T(8,128)(2,1)S(1)} %get-tuple-element.356), channel_id=1, source_target_pairs={{0,63},{1,0},{2,1},{3,2},{4,3},{5,4},{6,5},{7,6},{8,7},{9,8},{10,9... | collective-permute-start | bytes 1572872 | tf_op jit(solution)/shard_map/while/body/eval_jaxpr/ppermute | solution.py:10
  251.3 13.8 %collective-permute-start = (bf16[1,256,1024]{2,1,0:T(8,128)(2,1)S(1)}, bf16[1,256,1024]{2,1,0:T(8,128)(2,1)S(1)}, u32[]{:S(2)}, u32[]{:S(2)}) collective-permute-start(bf16[1,256,1024]{2,1,0:T(8,128)(2,1)S(1)} %get-tuple-element.356), channel_id=1, source_target_pairs={{0,63},{1,0},{2,1},{3,2},{4,3},{5,4},{6,5},{7,6},{8,7},{9,8},{10,9... | collective-permute-start | bytes 1572872 | tf_op jit(solution)/shard_map/while/body/eval_jaxpr/ppermute | solution.py:10
  270.3 13.8 %collective-permute-start = (bf16[1,256,1024]{2,1,0:T(8,128)(2,1)S(1)}, bf16[1,256,1024]{2,1,0:T(8,128)(2,1)S(1)}, u32[]{:S(2)}, u32[]{:S(2)}) collective-permute-start(bf16[1,256,1024]{2,1,0:T(8,128)(2,1)S(1)} %get-tuple-element.356), channel_id=1, source_target_pairs={{0,63},{1,0},{2,1},{3,2},{4,3},{5,4},{6,5},{7,6},{8,7},{9,8},{10,9... | collective-permute-start | bytes 1572872 | tf_op jit(solution)/shard_map/while/body/eval_jaxpr/ppermute | solution.py:10
  289.2 14.3 %collective-permute-start = (bf16[1,256,1024]{2,1,0:T(8,128)(2,1)S(1)}, bf16[1,256,1024]{2,1,0:T(8,128)(2,1)S(1)}, u32[]{:S(2)}, u32[]{:S(2)}) collective-permute-start(bf16[1,256,1024]{2,1,0:T(8,128)(2,1)S(1)} %get-tuple-element.356), channel_id=1, source_target_pairs={{0,63},{1,0},{2,1},{3,2},{4,3},{5,4},{6,5},{7,6},{8,7},{9,8},{10,9... | collective-permute-start | bytes 1572872 | tf_op jit(solution)/shard_map/while/body/eval_jaxpr/ppermute | solution.py:10
  308.6 15.3 %collective-permute-start = (bf16[1,256,1024]{2,1,0:T(8,128)(2,1)S(1)}, bf16[1,256,1024]{2,1,0:T(8,128)(2,1)S(1)}, u32[]{:S(2)}, u32[]{:S(2)}) collective-permute-start(bf16[1,256,1024]{2,1,0:T(8,128)(2,1)S(1)} %get-tuple-element.356), channel_id=1, source_target_pairs={{0,63},{1,0},{2,1},{3,2},{4,3},{5,4},{6,5},{7,6},{8,7},{9,8},{10,9... | collective-permute-start | bytes 1572872 | tf_op jit(solution)/shard_map/while/body/eval_jaxpr/ppermute | solution.py:10
  329.0 16.4 %collective-permute-start = (bf16[1,256,1024]{2,1,0:T(8,128)(2,1)S(1)}, bf16[1,256,1024]{2,1,0:T(8,128)(2,1)S(1)}, u32[]{:S(2)}, u32[]{:S(2)}) collective-permute-start(bf16[1,256,1024]{2,1,0:T(8,128)(2,1)S(1)} %get-tuple-element.356), channel_id=1, source_target_pairs={{0,63},{1,0},{2,1},{3,2},{4,3},{5,4},{6,5},{7,6},{8,7},{9,8},{10,9... | collective-permute-start | bytes 1572872 | tf_op jit(solution)/shard_map/while/body/eval_jaxpr/ppermute | solution.py:10
  350.6 17.5 %collective-permute-start = (bf16[1,256,1024]{2,1,0:T(8,128)(2,1)S(1)}, bf16[1,256,1024]{2,1,0:T(8,128)(2,1)S(1)}, u32[]{:S(2)}, u32[]{:S(2)}) collective-permute-start(bf16[1,256,1024]{2,1,0:T(8,128)(2,1)S(1)} %get-tuple-element.356), channel_id=1, source_target_pairs={{0,63},{1,0},{2,1},{3,2},{4,3},{5,4},{6,5},{7,6},{8,7},{9,8},{10,9... | collective-permute-start | bytes 1572872 | tf_op jit(solution)/shard_map/while/body/eval_jaxpr/ppermute | solution.py:10
  373.2 18.6 %collective-permute-start = (bf16[1,256,1024]{2,1,0:T(8,128)(2,1)S(1)}, bf16[1,256,1024]{2,1,0:T(8,128)(2,1)S(1)}, u32[]{:S(2)}, u32[]{:S(2)}) collective-permute-start(bf16[1,256,1024]{2,1,0:T(8,128)(2,1)S(1)} %get-tuple-element.356), channel_id=1, source_target_pairs={{0,63},{1,0},{2,1},{3,2},{4,3},{5,4},{6,5},{7,6},{8,7},{9,8},{10,9... | collective-permute-start | bytes 1572872 | tf_op jit(solution)/shard_map/while/body/eval_jaxpr/ppermute | solution.py:10
  396.9 19.2 %collective-permute-start = (bf16[1,256,1024]{2,1,0:T(8,128)(2,1)S(1)}, bf16[1,256,1024]{2,1,0:T(8,128)(2,1)S(1)}, u32[]{:S(2)}, u32[]{:S(2)}) collective-permute-start(bf16[1,256,1024]{2,1,0:T(8,128)(2,1)S(1)} %get-tuple-element.356), channel_id=1, source_target_pairs={{0,63},{1,0},{2,1},{3,2},{4,3},{5,4},{6,5},{7,6},{8,7},{9,8},{10,9... | collective-permute-start | bytes 1572872 | tf_op jit(solution)/shard_map/while/body/eval_jaxpr/ppermute | solution.py:10
  421.2 18.6 %collective-permute-start = (bf16[1,256,1024]{2,1,0:T(8,128)(2,1)S(1)}, bf16[1,256,1024]{2,1,0:T(8,128)(2,1)S(1)}, u32[]{:S(2)}, u32[]{:S(2)}) collective-permute-start(bf16[1,256,1024]{2,1,0:T(8,128)(2,1)S(1)} %get-tuple-element.356), channel_id=1, source_target_pairs={{0,63},{1,0},{2,1},{3,2},{4,3},{5,4},{6,5},{7,6},{8,7},{9,8},{10,9... | collective-permute-start | bytes 1572872 | tf_op jit(solution)/shard_map/while/body/eval_jaxpr/ppermute | solution.py:10
  444.9 17.7 %collective-permute-start = (bf16[1,256,1024]{2,1,0:T(8,128)(2,1)S(1)}, bf16[1,256,1024]{2,1,0:T(8,128)(2,1)S(1)}, u32[]{:S(2)}, u32[]{:S(2)}) collective-permute-start(bf16[1,256,1024]{2,1,0:T(8,128)(2,1)S(1)} %get-tuple-element.356), channel_id=1, source_target_pairs={{0,63},{1,0},{2,1},{3,2},{4,3},{5,4},{6,5},{7,6},{8,7},{9,8},{10,9... | collective-permute-start | bytes 1572872 | tf_op jit(solution)/shard_map/while/body/eval_jaxpr/ppermute | solution.py:10
  467.7 16.7 %collective-permute-start = (bf16[1,256,1024]{2,1,0:T(8,128)(2,1)S(1)}, bf16[1,256,1024]{2,1,0:T(8,128)(2,1)S(1)}, u32[]{:S(2)}, u32[]{:S(2)}) collective-permute-start(bf16[1,256,1024]{2,1,0:T(8,128)(2,1)S(1)} %get-tuple-element.356), channel_id=1, source_target_pairs={{0,63},{1,0},{2,1},{3,2},{4,3},{5,4},{6,5},{7,6},{8,7},{9,8},{10,9... | collective-permute-start | bytes 1572872 | tf_op jit(solution)/shard_map/while/body/eval_jaxpr/ppermute | solution.py:10
  489.6 15.8 %collective-permute-start = (bf16[1,256,1024]{2,1,0:T(8,128)(2,1)S(1)}, bf16[1,256,1024]{2,1,0:T(8,128)(2,1)S(1)}, u32[]{:S(2)}, u32[]{:S(2)}) collective-permute-start(bf16[1,256,1024]{2,1,0:T(8,128)(2,1)S(1)} %get-tuple-element.356), channel_id=1, source_target_pairs={{0,63},{1,0},{2,1},{3,2},{4,3},{5,4},{6,5},{7,6},{8,7},{9,8},{10,9... | collective-permute-start | bytes 1572872 | tf_op jit(solution)/shard_map/while/body/eval_jaxpr/ppermute | solution.py:10
  510.5 14.9 %collective-permute-start = (bf16[1,256,1024]{2,1,0:T(8,128)(2,1)S(1)}, bf16[1,256,1024]{2,1,0:T(8,128)(2,1)S(1)}, u32[]{:S(2)}, u32[]{:S(2)}) collective-permute-start(bf16[1,256,1024]{2,1,0:T(8,128)(2,1)S(1)} %get-tuple-element.356), channel_id=1, source_target_pairs={{0,63},{1,0},{2,1},{3,2},{4,3},{5,4},{6,5},{7,6},{8,7},{9,8},{10,9... | collective-permute-start | bytes 1572872 | tf_op jit(solution)/shard_map/while/body/eval_jaxpr/ppermute | solution.py:10
  530.5 14.1 %collective-permute-start = (bf16[1,256,1024]{2,1,0:T(8,128)(2,1)S(1)}, bf16[1,256,1024]{2,1,0:T(8,128)(2,1)S(1)}, u32[]{:S(2)}, u32[]{:S(2)}) collective-permute-start(bf16[1,256,1024]{2,1,0:T(8,128)(2,1)S(1)} %get-tuple-element.356), channel_id=1, source_target_pairs={{0,63},{1,0},{2,1},{3,2},{4,3},{5,4},{6,5},{7,6},{8,7},{9,8},{10,9... | collective-permute-start | bytes 1572872 | tf_op jit(solution)/shard_map/while/body/eval_jaxpr/ppermute | solution.py:10
  549.7 13.8 %collective-permute-start = (bf16[1,256,1024]{2,1,0:T(8,128)(2,1)S(1)}, bf16[1,256,1024]{2,1,0:T(8,128)(2,1)S(1)}, u32[]{:S(2)}, u32[]{:S(2)}) collective-permute-start(bf16[1,256,1024]{2,1,0:T(8,128)(2,1)S(1)} %get-tuple-element.356), channel_id=1, source_target_pairs={{0,63},{1,0},{2,1},{3,2},{4,3},{5,4},{6,5},{7,6},{8,7},{9,8},{10,9... | collective-permute-start | bytes 1572872 | tf_op jit(solution)/shard_map/while/body/eval_jaxpr/ppermute | solution.py:10
  587.6 13.8 %collective-permute-start = (bf16[1,256,1024]{2,1,0:T(8,128)(2,1)S(1)}, bf16[1,256,1024]{2,1,0:T(8,128)(2,1)S(1)}, u32[]{:S(2)}, u32[]{:S(2)}) collective-permute-start(bf16[1,256,1024]{2,1,0:T(8,128)(2,1)S(1)} %get-tuple-element.356), channel_id=1, source_target_pairs={{0,63},{1,0},{2,1},{3,2},{4,3},{5,4},{6,5},{7,6},{8,7},{9,8},{10,9... | collective-permute-start | bytes 1572872 | tf_op jit(solution)/shard_map/while/body/eval_jaxpr/ppermute | solution.py:10
  606.5 13.8 %collective-permute-start = (bf16[1,256,1024]{2,1,0:T(8,128)(2,1)S(1)}, bf16[1,256,1024]{2,1,0:T(8,128)(2,1)S(1)}, u32[]{:S(2)}, u32[]{:S(2)}) collective-permute-start(bf16[1,256,1024]{2,1,0:T(8,128)(2,1)S(1)} %get-tuple-element.356), channel_id=1, source_target_pairs={{0,63},{1,0},{2,1},{3,2},{4,3},{5,4},{6,5},{7,6},{8,7},{9,8},{10,9... | collective-permute-start | bytes 1572872 | tf_op jit(solution)/shard_map/while/body/eval_jaxpr/ppermute | solution.py:10
  625.5 13.8 %collective-permute-start = (bf16[1,256,1024]{2,1,0:T(8,128)(2,1)S(1)}, bf16[1,256,1024]{2,1,0:T(8,128)(2,1)S(1)}, u32[]{:S(2)}, u32[]{:S(2)}) collective-permute-start(bf16[1,256,1024]{2,1,0:T(8,128)(2,1)S(1)} %get-tuple-element.356), channel_id=1, source_target_pairs={{0,63},{1,0},{2,1},{3,2},{4,3},{5,4},{6,5},{7,6},{8,7},{9,8},{10,9... | collective-permute-start | bytes 1572872 | tf_op jit(solution)/shard_map/while/body/eval_jaxpr/ppermute | solution.py:10
  644.4 13.8 %collective-permute-start = (bf16[1,256,1024]{2,1,0:T(8,128)(2,1)S(1)}, bf16[1,256,1024]{2,1,0:T(8,128)(2,1)S(1)}, u32[]{:S(2)}, u32[]{:S(2)}) collective-permute-start(bf16[1,256,1024]{2,1,0:T(8,128)(2,1)S(1)} %get-tuple-element.356), channel_id=1, source_target_pairs={{0,63},{1,0},{2,1},{3,2},{4,3},{5,4},{6,5},{7,6},{8,7},{9,8},{10,9... | collective-permute-start | bytes 1572872 | tf_op jit(solution)/shard_map/while/body/eval_jaxpr/ppermute | solution.py:10
  663.4 13.8 %collective-permute-start = (bf16[1,256,1024]{2,1,0:T(8,128)(2,1)S(1)}, bf16[1,256,1024]{2,1,0:T(8,128)(2,1)S(1)}, u32[]{:S(2)}, u32[]{:S(2)}) collective-permute-start(bf16[1,256,1024]{2,1,0:T(8,128)(2,1)S(1)} %get-tuple-element.356), channel_id=1, source_target_pairs={{0,63},{1,0},{2,1},{3,2},{4,3},{5,4},{6,5},{7,6},{8,7},{9,8},{10,9... | collective-permute-start | bytes 1572872 | tf_op jit(solution)/shard_map/while/body/eval_jaxpr/ppermute | solution.py:10
  (7 other events, 697.6 us)
Sparse Core Ops, SparseCore 0:
  866.5 119.6 reduce-scatter.1
where the time goes:
time: 1000 us; the launch traced here: 997 us
  waiting for transfers between devices  337 us (34%)
  starting transfers between devices  253 us (25%)
  blocking collectives  155 us (16%)
  other arithmetic  118 us (12%)
  matrix products  85.5 us (9%)
  local copies, waits for them, and re-layouts  33.7 us (3%)
  between operations  13.4 us (1%)
    ppermute x32, starting transfers between devices, passed_along(): return lax.ppermute(value, axis, pairs)  253 us
    ppermute x32, waiting for transfers between devices, passed_along(): return lax.ppermute(value, axis, pairs)  217 us
    all_to_all x1, blocking collectives, local(): lax.all_to_all(out_abs, 'basis', split_axis=0, concat_axis=0, tiled=True)  155 us
    reduce_scatter x1, waiting for transfers between devices, local(): lax.psum_scatter(row_block.astype(jnp.bfloat16), 'rank', scatter_dimensio...  120 us
    dot_general x33, matrix products, pair_tile(): jnp.einsum('qmi,qni->mn', left, right, preferred_element_type=jnp.float32)  85.5 us
    scatter-add x32, other arithmetic, advance(): own_now = own_now.at[step].add(part * keep_own)  74 us
    another operation x32, other arithmetic  23 us
  transfers between devices with their start and end apart: 33, of which 33 were waited for; matrix products, arithmetic and copies ran while one was open for 2% of the time, Pallas kernels for 0%

commit v1 on v0

v1 whole, which is shorter than its diff:
```python
import functools

import jax
import jax.numpy as jnp
from jax import lax
from jax.experimental import pallas as pl
from jax.experimental.pallas import tpu as pltpu
from jax.sharding import PartitionSpec as P

MESH = pl.DeviceIdType.MESH
NY, NX, NZ = 4, 2, 8
ND = 5
F32, BF16 = jnp.float32, jnp.bfloat16


def kernel(
    src, out, rows_p, rows_q, dsend, drecv, acc, xsend, xrecv, direct, flipped,
    own_sem, p_ssem, p_rsem, q_ssem, q_rsem, d_ssem, d_rsem, x_ssem, x_rsem,
    a_ssem, a_rsem, b_ssem, b_rsem, l_sem,
):
    rank = lax.axis_index("rank")
    basis = lax.axis_index("basis")
    lo, core = rank // 2, rank % 2
    z = basis % NZ
    xh = (basis // NZ) % NX
    y = basis // (NZ * NX)

    def at(y_, x_, z_):
        return (y_ * NX + x_) * NZ + z_

    other_core = (lo * 2 + (1 - core), basis)
    other_lo = ((1 - lo) * 2 + core, basis)
    other_x = (rank, at(y, 1 - xh, z))
    y_up = (rank, at((y + 1) % NY, xh, z))
    y_down = (rank, at((y + 3) % NY, xh, z))
    z_down = (rank, at(y, xh, (z + NZ - 1) % NZ))

    def z_off(d):
        return (rank, at(y, xh, (z + d) % NZ))

    def columns(x_, z_):
        width = src.shape[0]
        start = pl.multiple_of((x_ * NZ + z_) * width, width)
        return out.at[:, pl.ds(start, width)]

    def mirror(x_):
        return (y, at(rank, x_, z))

    barrier = pltpu.get_barrier_semaphore()
    partners = [other_core, other_lo, other_x, y_up, y_down]
    partners += [z_off(d) for d in (1, 2, 3, 5, 6, 7)]
    for who in partners:
        pl.semaphore_signal(barrier, inc=1, device_id=who, device_id_type=MESH)

    @pl.when(rank != y)
    def _():
        for x_ in range(NX):
            pl.semaphore_signal(
                barrier, inc=1, device_id=mirror(x_), device_id_type=MESH
            )

    pl.semaphore_wait(barrier, len(partners) + jnp.where(rank != y, NX, 0))

    def remote(a, b, ssem, rsem, who):
        return pltpu.make_async_remote_copy(
            src_ref=a, dst_ref=b, send_sem=ssem, recv_sem=rsem,
            device_id=who, device_id_type=MESH,
        )

    def p_copy(d):
        a = src if d == 0 else rows_p.at[d]
        return remote(a, rows_p.at[d + 1], p_ssem.at[d], p_rsem.at[d + 1], z_down)

    def q_slot(dy, flip):
        return ((y + dy) % NY) * NX + (xh + flip) % NX

    def q_copy(i, dy, flip, who):
        slot = q_slot(dy, flip)
        a = src if (dy, flip) == (0, 0) else rows_q.at[slot]
        return remote(a, rows_q.at[slot], q_ssem.at[i], q_rsem.at[slot], who)

    def q_wait(dy, flip):
        slot = q_slot(dy, flip)
        remote(
            src, rows_q.at[slot], q_ssem.at[0], q_rsem.at[slot], other_x
        ).wait_recv()

    def p_wait(d):
        remote(src, rows_p.at[d], p_ssem.at[0], p_rsem.at[d], z_down).wait_recv()

    p_sends = [p_copy(d) for d in range(ND - 1)]
    q_sends = [
        q_copy(0, 0, 0, y_up),
        q_copy(1, 0, 0, y_down),
        q_copy(2, 0, 0, other_x),
        q_copy(3, 0, 1, y_up),
        q_copy(4, 0, 1, y_down),
        q_copy(5, 1, 0, y_down),
        q_copy(6, 3, 1, y_up),
    ]
    p_sends[0].start()
    q_sends[0].start()
    q_sends[1].start()
    q_sends[2].start()
    own_p = pltpu.make_async_copy(src, rows_p.at[0], own_sem.at[0])
    own_q = pltpu.make_async_copy(src, rows_q.at[q_slot(0, 0)], own_sem.at[1])
    own_p.start()
    own_q.start()
    own_p.wait()
    own_q.wait()

    def unit(g, h):
        m = ((g + 1) // 2) % 2
        dy = (g + 1) // 2 + 2 * m * h
        flip = m * (g // 2) + (1 - m) * h
        return (y + dy) % NY, (xh + flip) % NX

    def each(g0, g1, d0, d1, body):
        nd = d1 - d0

        def step(k, carry):
            d = d0 + k % nd
            rest = k // nd
            yc, xc = unit(g0 + rest // 2, rest % 2)
            body(d, yc, xc)
            return carry

        lax.fori_loop(0, (g1 - g0) * 2 * nd, step, 0)

    def d_copy(d, yc, xc):
        s = ((yc // 2) * NX + xc) * ND + d
        return remote(dsend.at[s], drecv.at[s], d_ssem.at[s], d_rsem.at[s], other_core)

    def x_copy(d, xc):
        s = xc * ND + d
        return remote(xsend.at[s], xrecv.at[s], x_ssem.at[s], x_rsem.at[s], other_lo)

    def a_copy(d, xc):
        s = xc * ND + d
        return remote(
            direct.at[s], columns(xc, z), a_ssem.at[s], a_rsem.at[s], z_off(d)
        )

    def b_copy(d, xc):
        s, r = xc * ND + d, xh * ND + d
        return remote(
            flipped.at[s], columns(xh, (z + d) % NZ), b_ssem.at[s], b_rsem.at[r],
            mirror(xc),
        )

    def b_local(d, xc):
        s, r = xc * ND + d, xh * ND + d
        return pltpu.make_async_copy(
            flipped.at[s], columns(xh, (z + d) % NZ), b_rsem.at[r]
        )

    def a_local(xc):
        return pltpu.make_async_copy(
            direct.at[xc * ND], columns(xc, z), l_sem.at[xc]
        )

    def to_self(xc):
        return jnp.logical_and(rank == y, xc == xh)

    def multiply(d, yc, xc):
        s = ((yc // 2) * NX + xc) * ND + d
        t = lax.dot_general(
            rows_p[d], rows_q[yc * NX + xc], (((1,), (1,)), ((), ())),
            preferred_element_type=F32,
        )

        @pl.when(yc % 2 != core)
        def _():
            dsend[s] = t.astype(BF16)
            d_copy(d, yc, xc).start()

        @pl.when(yc % 2 == core)
        def _():
            acc[s] = t

    def pass_on(d, yc, xc):
        s = ((yc // 2) * NX + xc) * ND + d

        @pl.when(jnp.logical_and(yc % 2 == core, yc // 2 != lo))
        def _():
            d_copy(d, yc, xc).wait_recv()
            xsend[xc * ND + d] = (acc[s] + drecv[s].astype(F32)).astype(BF16)
            x_copy(d, xc).start()

    def finish(d, yc, xc):
        s = ((yc // 2) * NX + xc) * ND + d
        e = xc * ND + d

        @pl.when(yc == rank)
        def _():
            d_copy(d, yc, xc).wait_recv()
            x_copy(d, xc).wait_recv()
            v = acc[s] + drecv[s].astype(F32) + xrecv[e].astype(F32)

            @pl.when(d < ND - 1)
            def _():
                direct[e] = v.astype(BF16)

            @pl.when(d == 0)
            def _():
                a_local(xc).start()

            @pl.when(jnp.logical_and(d > 0, d < ND - 1))
            def _():
                a_copy(d, xc).start()

            @pl.when(d > 0)
            def _():
                flipped[e] = v.T.astype(BF16)

                @pl.when(to_self(xc))
                def _():
                    b_local(d, xc).start()

                @pl.when(jnp.logical_not(to_self(xc)))
                def _():
                    b_copy(d, xc).start()

    def run(*boxes):
        for body in (multiply, pass_on, finish):
            for g0, g1, d0, d1 in boxes:
                each(g0, g1, d0, d1, body)

    p_wait(1)
    p_sends[1].start()
    q_wait(0, 1)
    q_sends[3].start()
    q_sends[4].start()
    q_wait(1, 0)
    q_sends[5].start()
    q_wait(3, 0)
    run((0, 2, 0, 2))
    p_wait(2)
    p_sends[2].start()
    q_wait(3, 1)
    q_sends[6].start()
    q_wait(1, 1)
    run((0, 2, 2, 3), (2, 3, 0, 3))
    p_wait(3)
    p_sends[3].start()
    q_wait(2, 0)
    q_wait(2, 1)
    run((0, 3, 3, 4), (3, 4, 0, 4))
    p_wait(4)
    run((0, 4, 4, 5))

    for c in p_sends + q_sends:
        c.wait_send()

    def drain(d, yc, xc):
        @pl.when(yc % 2 != core)
        def _():
            d_copy(d, yc, xc).wait_send()

        @pl.when(jnp.logical_and(yc % 2 == core, yc // 2 != lo))
        def _():
            x_copy(d, xc).wait_send()

        @pl.when(yc == rank)
        def _():
            @pl.when(d == 0)
            def _():
                a_local(xc).wait()

            @pl.when(jnp.logical_and(d > 0, d < ND - 1))
            def _():
                a_copy(d, xc).wait()

            @pl.when(d > 0)
            def _():

                @pl.when(jnp.logical_not(to_self(xc)))
                def _():
                    b_copy(d, xc).wait_send()

    each(0, 4, 0, ND, drain)

    def landed(k, carry):
        d, xs = 1 + k % (ND - 1), k // (ND - 1)
        pltpu.make_async_copy(
            flipped.at[xs * ND + d], columns(xs, (z + d) % NZ), b_rsem.at[xs * ND + d]
        ).wait()
        return carry

    lax.fori_loop(0, NX * (ND - 1), landed, 0)


def solution(mesh):
    def local(factors):
        _, rows, depth = factors.shape
        tile = (rows, rows)
        n = NX * ND
        dma = pltpu.SemaphoreType.DMA
        blocks = pl.pallas_call(
            kernel,
            out_shape=jax.ShapeDtypeStruct((rows, NX * NZ * rows), BF16),
            in_specs=[pl.BlockSpec(memory_space=pl.ANY)],
            out_specs=pl.BlockSpec(memory_space=pl.ANY),
            scratch_shapes=[
                pltpu.VMEM((ND, rows, depth), BF16),
                pltpu.VMEM((NY * NX, rows, depth), BF16),
                pltpu.VMEM((2 * n, *tile), BF16),
                pltpu.VMEM((2 * n, *tile), BF16),
                pltpu.VMEM((2 * n, *tile), F32),
                pltpu.VMEM((n, *tile), BF16),
                pltpu.VMEM((n, *tile), BF16),
                pltpu.VMEM((n, *tile), BF16),
                pltpu.VMEM((n, *tile), BF16),
                dma((2,)),
                dma((ND,)), dma((ND,)),
                dma((7,)), dma((NY * NX,)),
                dma((2 * n,)), dma((2 * n,)),
                dma((n,)), dma((n,)),
                dma((n,)), dma((n,)),
                dma((n,)), dma((n,)),
                dma((NX,)),
            ],
            compiler_params=pltpu.CompilerParams(
                collective_id=0, has_side_effects=True, vmem_limit_bytes=40 * 2**20
            ),
        )(factors[0])
        return blocks.astype(F32)

    return jax.shard_map(
        local,
        mesh=mesh,
        in_specs=(P("rank", "basis", None),),
        out_specs=P("basis", "rank"),
        check_vma=False,
    )
```

time: 1000 us -> 96.9 us (0.10)
  waiting for transfers between devices: 337 us -> 0 us
  starting transfers between devices: 253 us -> 0 us
  blocking collectives: 155 us -> 0 us
  other arithmetic: 118 us -> 2.51 us
  Pallas kernels: 0 us -> 93.2 us
  matrix products: 85.5 us -> 0 us
  local copies, waits for them, and re-layouts: 33.7 us -> 1.04 us
  between operations: 13.4 us -> 0.01 us
    ppermute x32 -> x0, starting transfers between devices: 253 us -> none  [passed_along(): return lax.ppermute(value, axis, pairs)]
    ppermute x32 -> x0, waiting for transfers between devices: 217 us -> none  [passed_along(): return lax.ppermute(value, axis, pairs)]
    all_to_all x1 -> x0, blocking collectives: 155 us -> none  [local(): lax.all_to_all(out_abs, 'basis', split_axis=0, concat_axis=0, tiled=True)]
    reduce_scatter x1 -> x0, waiting for transfers between devices: 120 us -> none  [local(): lax.psum_scatter(row_block.astype(jnp.bfloat16), 'rank', scatter_dimensio...]
    pallas_call x0 -> x1, Pallas kernels: none -> 93.2 us  [local(): pl.pallas_call(kernel, out_shape=jax.ShapeDtypeStruct((rows, NX * NZ * ro...]
    dot_general x33 -> x0, matrix products: 85.5 us -> none  [pair_tile(): jnp.einsum('qmi,qni->mn', left, right, preferred_element_type=jnp.float32)]
    scatter-add x32 -> x0, other arithmetic: 74 us -> none  [advance(): own_now = own_now.at[step].add(part * keep_own)]
    another operation x32 -> x0, other arithmetic: 23 us -> none
  transfers between devices with their start and end apart: 33 -> 0, of which waited for: 33 -> 0; matrix products, arithmetic and copies ran while one was open for 2% -> 0% of each run, Pallas kernels for 0% -> 0%
where the time goes in v1:
time: 96.9 us; the launch traced here: 96.7 us
  Pallas kernels  93.2 us (96%)
  other arithmetic  2.51 us (3%)
  local copies, waits for them, and re-layouts  1.04 us (1%)
    pallas_call x1, Pallas kernels, local(): pl.pallas_call(kernel, out_shape=jax.ShapeDtypeStruct((rows, NX * NZ * ro...  93.2 us
    convert_element_type x1, other arithmetic, local(): return blocks.astype(F32)  2.51 us

profile of v1, /device:TPU:1, one launch (start us, length us, event | category | flops | bytes accessed | tf_op | source)
XLA Modules:
  0.0 96.7 jit_solution(14278492877137719834)
XLA Ops:
  0.0 0.0 copy-start
  0.0 1.0 %copy-done = bf16[1,256,1024]{2,1,0:T(8,128)(2,1)S(1)} copy-done((bf16[1,256,1024]{2,1,0:T(8,128)(2,1)S(1)}, bf16[1,256,1024]{2,1,0:T(8,128)(2,1)}, u32[]{:S(2)}) %copy-start) | copy-done | bytes 524312
  1.0 93.2 %shard_map.17 = bf16[256,4096]{1,0:T(8,128)(2,1)S(1)} custom-call(bf16[256,1024]{1,0:T(8,128)(2,1)S(1)} %bitcast.1), custom_call_target="tpu_custom_call" | custom-call | tf_op jit(solution)/shard_map/pallas_call | solution.py:299
  94.2 2.5 %convert_element_type.3 = f32[256,4096]{1,0:T(8,128)} convert(bf16[256,4096]{1,0:T(8,128)(2,1)S(1)} %shard_map.17) | non-fusion elementwise | flops 1048576 | bytes 6291456 | tf_op jit(solution)/shard_map/convert_element_type | solution.py:327
Async XLA Ops:
  0.0 1.0 %copy-start = (bf16[1,256,1024]{2,1,0:T(8,128)(2,1)S(1)}, bf16[1,256,1024]{2,1,0:T(8,128)(2,1)}, u32[]{:S(2)}) copy-start(bf16[1,256,1024]{2,1,0:T(8,128)(2,1)} %param.1) | copy-start | bytes 1572868

commit v2 on v1

v2 whole, which is shorter than its diff:
```python
import functools

import jax
import jax.numpy as jnp
from jax import lax
from jax.experimental import pallas as pl
from jax.experimental.pallas import tpu as pltpu
from jax.sharding import PartitionSpec as P

MESH = pl.DeviceIdType.MESH
NY, NX, NZ = 4, 2, 8
F32, BF16 = jnp.float32, jnp.bfloat16

NQ, ND = NY * NX, 5

def both(*pairs):
    return tuple((q, d) for p, d in pairs for q in (p, p + 1))


FIRST = both((0, 1), (0, 0)) + ((2, 1), (6, 1))
SECOND = both((6, 2), (0, 2), (6, 0)) + ((4, 2), (4, 1), (7, 1), (2, 2))
THIRD = both((0, 3), (2, 3), (4, 3), (6, 3))
LATE = ((3, 2), (5, 2), (3, 1), (5, 1))
KEPT = both((2, 0), (4, 0))
LAST = both((0, 4), (2, 4), (4, 4), (6, 4))
STEPS = (FIRST, SECOND, THIRD, LATE, KEPT, LAST)


def kernel(
    src, out, rows, dsend, drecv, acc, xsend, xrecv, direct, flipped,
    own_sem, p_ssem, p_rsem, q_ssem, q_rsem, d_ssem, d_rsem, x_ssem, x_rsem,
    a_ssem, a_rsem, b_ssem, b_rsem,
):
    rank = lax.axis_index("rank")
    basis = lax.axis_index("basis")
    lo, core = rank // 2, rank % 2
    z = basis % NZ
    xh = (basis // NZ) % NX
    y = basis // (NZ * NX)

    def at(y_, x_, z_):
        return (y_ * NX + x_) * NZ + z_

    other_core = (lo * 2 + (1 - core), basis)
    other_lo = ((1 - lo) * 2 + core, basis)
    other_x = (rank, at(y, 1 - xh, z))
    beside = ((1 - lo) * 2 + core, at(y, 1 - xh, z))
    y_up = (rank, at((y + 1) % NY, xh, z))
    y_down = (rank, at((y + 3) % NY, xh, z))

    def z_off(d):
        return (rank, at(y, xh, (z + d) % NZ))

    z_up, z_down = z_off(1), z_off(NZ - 1)

    half = src.shape[0] // 2

    def columns(x_, z_):
        width = src.shape[0]
        start = pl.multiple_of((x_ * NZ + z_) * width, width)
        return out.at[:, pl.ds(start, width)]

    def mirror(x_):
        return (y, at(rank, x_, z))

    barrier = pltpu.get_barrier_semaphore()
    partners = [other_core, other_lo, other_x, beside, y_up, y_down]
    partners += [z_off(d) for d in (1, 2, 3, 5, 6, 7)]
    for who in partners:
        pl.semaphore_signal(barrier, inc=1, device_id=who, device_id_type=MESH)

    @pl.when(rank != y)
    def _():
        for x_ in range(NX):
            pl.semaphore_signal(
                barrier, inc=1, device_id=mirror(x_), device_id_type=MESH
            )

    pl.semaphore_wait(barrier, len(partners) + jnp.where(rank != y, NX, 0))

    def remote(a, b, ssem, rsem, who):
        return pltpu.make_async_remote_copy(
            src_ref=a, dst_ref=b, send_sem=ssem, recv_sem=rsem,
            device_id=who, device_id_type=MESH,
        )

    def p_block(d):
        return src if d == 0 else rows.at[NQ + d - 1]

    def p_down(d):
        a, b = p_block(d), p_block(d + 1)
        if d == 3:
            a, b = a.at[pl.ds(0, half)], b.at[pl.ds(0, half)]
        return remote(a, b, p_ssem.at[d], p_rsem.at[d], z_down)

    def p_up(d):
        a, b = p_block((NZ - d) % NZ), p_block(NZ - d - 1)
        if d == 3:
            a, b = a.at[pl.ds(half, half)], b.at[pl.ds(half, half)]
        return remote(a, b, p_ssem.at[4 + d], p_rsem.at[4 + d], z_up)

    def q_slot(dy, flip):
        return ((y + dy) % NY) * NX + (xh + flip) % NX

    def q_copy(i, dy, flip, who):
        slot = q_slot(dy, flip)
        a = src if (dy, flip) == (0, 0) else rows.at[slot]
        return remote(a, rows.at[slot], q_ssem.at[i], q_rsem.at[slot], who)

    def q_wait(dy, flip):
        slot = q_slot(dy, flip)
        remote(
            src, rows.at[slot], q_ssem.at[0], q_rsem.at[slot], other_x
        ).wait_recv()

    down = [p_down(d) for d in range(4)]
    up = [p_up(d) for d in range(4)]
    q_sends = [
        q_copy(0, 0, 0, y_down),
        q_copy(1, 0, 0, y_up),
        q_copy(2, 0, 0, other_x),
        q_copy(3, 1, 0, y_down),
        q_copy(4, 0, 1, y_up),
        q_copy(5, 0, 1, y_down),
        q_copy(6, 3, 1, y_up),
    ]
    down[0].start()
    up[0].start()
    q_sends[0].start()
    q_sends[1].start()
    q_sends[2].start()
    own = pltpu.make_async_copy(src, rows.at[q_slot(0, 0)], own_sem.at[0])
    own.start()
    own.wait()

    def each(units, body):
        for first in range(0, len(units), 10):
            part = units[first : first + 10]
            qs = sum(q * 8**k for k, (q, _) in enumerate(part))
            ds = sum(d * 8**k for k, (_, d) in enumerate(part))

            def step(k, carry):
                qs, ds = carry
                body(qs % 8, ds % 8)
                return qs // 8, ds // 8

            lax.fori_loop(0, len(part), step, (jnp.int32(qs), jnp.int32(ds)))

    def block(q):
        return (y + q // 2) % NY, (xh + q % 2) % NX

    def full(yc, xc, d):
        return ((yc // 2) * NX + xc) * ND + d

    def d_copy(s):
        return remote(dsend.at[s], drecv.at[s], d_ssem.at[s], d_rsem.at[s], other_core)

    def x_copy(d, xc):
        e = xc * ND + d
        to = ((1 - lo) * 2 + core, at(y, jnp.where(d == 0, 1 - xh, xh), z))
        return remote(xsend.at[e], xrecv.at[e], x_ssem.at[e], x_rsem.at[e], to)

    def away(yc, d):
        return jnp.where((yc + y) % 2 == 0, d, (NZ - d) % NZ)

    def a_copy(d, xc):
        e = xc * ND + d
        return remote(
            direct.at[e], columns(xc, z), a_ssem.at[e], a_rsem.at[e],
            z_off(away(rank, d)),
        )

    def a_local(xc):
        e = xc * ND
        return pltpu.make_async_copy(direct.at[e], columns(xc, z), a_rsem.at[e])

    def b_place(d, x_):
        return columns(x_, (z + away(rank, d)) % NZ)

    def b_copy(d, xc):
        e, r = xc * ND + d, xh * ND + d
        return remote(
            flipped.at[e], b_place(d, xh), b_ssem.at[e], b_rsem.at[r], mirror(xc)
        )

    def b_local(d, x_):
        e = x_ * ND + d
        return pltpu.make_async_copy(flipped.at[e], b_place(d, x_), b_rsem.at[e])

    def goes_direct(q, d):
        return d < ND - 1

    def goes_flipped(q, d):
        return d > 0

    def left(yc, d):
        side = jnp.where(yc // 2 == lo, xh, 1 - xh)
        return rows[jnp.where(d == 0, y * NX + side, NQ + away(yc, d) - 1)]

    def place(t, yc, xc, d):
        s = full(yc, xc, d)

        @pl.when(yc % 2 != core)
        def _():
            dsend[s] = t.astype(BF16)
            d_copy(s).start()

        @pl.when(yc % 2 == core)
        def _():
            acc[s] = t

    def product(a, b):
        return lax.dot_general(
            a, b, (((1,), (1,)), ((), ())), preferred_element_type=F32
        )

    def multiply(q, d):
        yc, xc = block(q)
        place(product(left(yc, d), rows[yc * NX + xc]), yc, xc, d)

    def multiply_both(yc, d):
        n, depth = src.shape
        b = rows[pl.ds(yc * NX, NX)].reshape(NX * n, depth)
        t = product(left(yc, d), b)
        for xc in range(NX):
            place(t[:, xc * n : (xc + 1) * n], yc, xc, d)

    def pairs(todo):
        each(todo, lambda q, d: multiply_both((y + q // 2) % NY, d))

    def all_pairs(d):
        def step(k, carry):
            multiply_both(((k // 2 + 1 + lo) % 2) * 2 + k % 2, d)
            return carry

        lax.fori_loop(0, NY, step, 0)

    def pass_on(q, d):
        yc, xc = block(q)
        s, e = full(yc, xc, d), xc * ND + d

        @pl.when(jnp.logical_and(yc % 2 == core, yc // 2 != lo))
        def _():
            d_copy(s).wait_recv()
            xsend[e] = (acc[s] + drecv[s].astype(F32)).astype(BF16)
            x_copy(d, xc).start()

    def finish(q, d):
        yc, xc = block(q)
        s, e = full(yc, xc, d), xc * ND + d

        @pl.when(yc == rank)
        def _():
            d_copy(s).wait_recv()
            x_copy(d, xc).wait_recv()
            v = acc[s] + drecv[s].astype(F32) + xrecv[e].astype(F32)

            @pl.when(goes_direct(q, d))
            def _():
                direct[e] = v.astype(BF16)

                @pl.when(d == 0)
                def _():
                    a_local(xc).start()

                @pl.when(d > 0)
                def _():
                    a_copy(d, xc).start()

            @pl.when(goes_flipped(q, d))
            def _():
                flipped[e] = v.T.astype(BF16)

                @pl.when(q == 0)
                def _():
                    b_local(d, xh).start()

                @pl.when(q > 0)
                def _():
                    b_copy(d, xc).start()

    down[0].wait_recv()
    down[1].start()
    up[0].wait_recv()
    up[1].start()
    q_wait(0, 1)
    q_sends[4].start()
    q_wait(1, 0)
    q_sends[3].start()
    q_sends[5].start()
    pairs(((0, 1), (0, 0)))
    q_wait(3, 0)
    each(((2, 1), (6, 1)), multiply)
    each(FIRST, pass_on)
    each(FIRST, finish)

    down[1].wait_recv()
    down[2].start()
    up[1].wait_recv()
    up[2].start()
    q_wait(3, 1)
    q_sends[6].start()
    pairs(((6, 2), (0, 2)))
    q_wait(2, 0)
    each(((4, 2), (4, 1), (7, 1), (2, 2)), multiply)
    each(SECOND[:4], pass_on)
    pairs(((6, 0),))
    each(SECOND[4:], pass_on)

    down[2].wait_recv()
    down[3].start()
    up[2].wait_recv()
    up[3].start()
    each(SECOND, finish)
    q_wait(1, 1)
    q_wait(2, 1)
    all_pairs(3)
    each(THIRD, pass_on)
    each(LATE, multiply)
    each(LATE, pass_on)
    pairs(((2, 0), (4, 0)))
    each(KEPT, pass_on)
    each(THIRD, finish)

    down[3].wait_recv()
    up[3].wait_recv()
    all_pairs(4)
    each(LAST, pass_on)
    for units in (LATE, LAST, KEPT):
        each(units, finish)

    for c in down + up + q_sends:
        c.wait_send()

    def drain(q, d):
        yc, xc = block(q)

        @pl.when(yc % 2 != core)
        def _():
            d_copy(full(yc, xc, d)).wait_send()

        @pl.when(jnp.logical_and(yc % 2 == core, yc // 2 != lo))
        def _():
            x_copy(d, xc).wait_send()

        @pl.when(yc == rank)
        def _():
            @pl.when(goes_direct(q, d))
            def _():
                @pl.when(d == 0)
                def _():
                    a_local(xc).wait()

                @pl.when(d > 0)
                def _():
                    a_copy(d, xc).wait()

            @pl.when(jnp.logical_and(q > 0, goes_flipped(q, d)))
            def _():
                b_copy(d, xc).wait_send()

        @pl.when(jnp.logical_and((rank + q // 2) % NY == y, goes_flipped(q, d)))
        def _():
            b_local(d, (xh + q) % NX).wait()

    for units in STEPS:
        each(units, drain)


def solution(mesh):
    def local(factors):
        _, rows, depth = factors.shape
        tile = (rows, rows)
        n = NX * ND
        dma = pltpu.SemaphoreType.DMA
        blocks = pl.pallas_call(
            kernel,
            out_shape=jax.ShapeDtypeStruct((rows, NX * NZ * rows), BF16),
            in_specs=[pl.BlockSpec(memory_space=pl.ANY)],
            out_specs=pl.BlockSpec(memory_space=pl.ANY),
            scratch_shapes=[
                pltpu.VMEM((NQ + NZ - 1, rows, depth), BF16),
                pltpu.VMEM((2 * n, *tile), BF16),
                pltpu.VMEM((2 * n, *tile), BF16),
                pltpu.VMEM((2 * n, *tile), F32),
                pltpu.VMEM((n, *tile), BF16),
                pltpu.VMEM((n, *tile), BF16),
                pltpu.VMEM((n, *tile), BF16),
                pltpu.VMEM((n, *tile), BF16),
                dma((1,)),
                dma((NZ,)), dma((NZ,)),
                dma((7,)), dma((NQ,)),
                dma((2 * n,)), dma((2 * n,)),
                dma((n,)), dma((n,)),
                dma((n,)), dma((n,)),
                dma((n,)), dma((n,)),
            ],
            compiler_params=pltpu.CompilerParams(
                collective_id=0, has_side_effects=True, vmem_limit_bytes=44 * 2**20
            ),
        )(factors[0])
        return blocks.astype(F32)

    return jax.shard_map(
        local,
        mesh=mesh,
        in_specs=(P("rank", "basis", None),),
        out_specs=P("basis", "rank"),
        check_vma=False,
    )
```

time: 96.9 us -> 87.2 us (0.90); the launches traced: 96.7 us -> 85.7 us
  Pallas kernels: 93.2 us -> 82.1 us
    pallas_call x1, Pallas kernels: 93.2 us -> 82.1 us  [local(): pl.pallas_call(kernel, out_shape=jax.ShapeDtypeStruct((rows, NX * NZ * ro...]
where the time goes in v2:
time: 87.2 us; the launch traced here: 85.7 us
  Pallas kernels  82.1 us (94%)
  other arithmetic  2.51 us (3%)
  local copies, waits for them, and re-layouts  1.04 us (1%)
    pallas_call x1, Pallas kernels, local(): pl.pallas_call(kernel, out_shape=jax.ShapeDtypeStruct((rows, NX * NZ * ro...  82.1 us
    convert_element_type x1, other arithmetic, local(): return blocks.astype(F32)  2.51 us

profile of v2, /device:TPU:1, one launch (start us, length us, event | category | flops | bytes accessed | tf_op | source)
XLA Modules:
  0.0 85.7 jit_solution(18087413585912875694)
XLA Ops:
  0.0 0.0 copy-start
  0.0 1.0 %copy-done = bf16[1,256,1024]{2,1,0:T(8,128)(2,1)S(1)} copy-done((bf16[1,256,1024]{2,1,0:T(8,128)(2,1)S(1)}, bf16[1,256,1024]{2,1,0:T(8,128)(2,1)}, u32[]{:S(2)}) %copy-start) | copy-done | bytes 524312
  1.0 82.1 %shard_map.17 = bf16[256,4096]{1,0:T(8,128)(2,1)S(1)} custom-call(bf16[256,1024]{1,0:T(8,128)(2,1)S(1)} %bitcast.1), custom_call_target="tpu_custom_call" | custom-call | tf_op jit(solution)/shard_map/pallas_call | solution.py:376
  83.2 2.5 %convert_element_type.3 = f32[256,4096]{1,0:T(8,128)} convert(bf16[256,4096]{1,0:T(8,128)(2,1)S(1)} %shard_map.17) | non-fusion elementwise | flops 1048576 | bytes 6291456 | tf_op jit(solution)/shard_map/convert_element_type | solution.py:402
Async XLA Ops:
  0.0 1.0 %copy-start = (bf16[1,256,1024]{2,1,0:T(8,128)(2,1)S(1)}, bf16[1,256,1024]{2,1,0:T(8,128)(2,1)}, u32[]{:S(2)}) copy-start(bf16[1,256,1024]{2,1,0:T(8,128)(2,1)} %param.1) | copy-start | bytes 1572868

commit v3 on v2

--- a/solution.py
+++ b/solution.py
@@ -18,12 +18,12 @@
 
 
 FIRST = both((0, 1), (0, 0)) + ((2, 1), (6, 1))
-SECOND = both((6, 2), (0, 2), (6, 0)) + ((4, 2), (4, 1), (7, 1), (2, 2))
+SECOND = both((2, 2), (6, 2), (0, 2)) + ((3, 1), (7, 1), (4, 2), (4, 1)) + both((6, 0))
+LATE = ((5, 2), (5, 1))
 THIRD = both((0, 3), (2, 3), (4, 3), (6, 3))
-LATE = ((3, 2), (5, 2), (3, 1), (5, 1))
 KEPT = both((2, 0), (4, 0))
 LAST = both((0, 4), (2, 4), (4, 4), (6, 4))
-STEPS = (FIRST, SECOND, THIRD, LATE, KEPT, LAST)
+STEPS = (FIRST, SECOND, LATE, THIRD, KEPT, LAST)
 
 
 def kernel(
@@ -102,15 +102,25 @@
     def q_slot(dy, flip):
         return ((y + dy) % NY) * NX + (xh + flip) % NX
 
-    def q_copy(i, dy, flip, who):
-        slot = q_slot(dy, flip)
-        a = src if (dy, flip) == (0, 0) else rows.at[slot]
-        return remote(a, rows.at[slot], q_ssem.at[i], q_rsem.at[slot], who)
+    def q_copy(i, dy, flip, who, part=None):
+        at_slot = rows.at[q_slot(dy, flip)]
+        a = src if (dy, flip) == (0, 0) else at_slot
+        sem = q_slot(dy, flip)
+        if part is not None:
+            a, at_slot = (r.at[pl.ds(part * half, half)] for r in (a, at_slot))
+            sem = NQ + part
+        return remote(a, at_slot, q_ssem.at[i], q_rsem.at[sem], who)
 
     def q_wait(dy, flip):
         slot = q_slot(dy, flip)
         remote(
             src, rows.at[slot], q_ssem.at[0], q_rsem.at[slot], other_x
+        ).wait_recv()
+
+    def q_wait_part(dy, flip, part):
+        place = rows.at[q_slot(dy, flip), pl.ds(part * half, half)]
+        remote(
+            src.at[pl.ds(0, half)], place, q_ssem.at[0], q_rsem.at[NQ + part], other_x
         ).wait_recv()
 
     down = [p_down(d) for d in range(4)]
@@ -120,9 +130,10 @@
         q_copy(1, 0, 0, y_up),
         q_copy(2, 0, 0, other_x),
         q_copy(3, 1, 0, y_down),
-        q_copy(4, 0, 1, y_up),
-        q_copy(5, 0, 1, y_down),
-        q_copy(6, 3, 1, y_up),
+        q_copy(4, 1, 0, other_x),
+        q_copy(5, 0, 1, y_up),
+        q_copy(6, 1, 1, y_down, 0),
+        q_copy(7, 3, 1, y_up, 1),
     ]
     down[0].start()
     up[0].start()
@@ -284,40 +295,44 @@
     up[0].wait_recv()
     up[1].start()
     q_wait(0, 1)
-    q_sends[4].start()
+    q_sends[5].start()
     q_wait(1, 0)
     q_sends[3].start()
-    q_sends[5].start()
+    q_sends[4].start()
     pairs(((0, 1), (0, 0)))
     q_wait(3, 0)
     each(((2, 1), (6, 1)), multiply)
     each(FIRST, pass_on)
-    each(FIRST, finish)
 
     down[1].wait_recv()
     down[2].start()
     up[1].wait_recv()
     up[2].start()
     q_wait(3, 1)
+    q_sends[7].start()
+    q_wait(1, 1)
     q_sends[6].start()
-    pairs(((6, 2), (0, 2)))
+    pairs(((2, 2), (6, 2), (0, 2)))
+    each(SECOND[:6], pass_on)
     q_wait(2, 0)
-    each(((4, 2), (4, 1), (7, 1), (2, 2)), multiply)
-    each(SECOND[:4], pass_on)
+    each(SECOND[6:10], multiply)
+    each(SECOND[6:10], pass_on)
     pairs(((6, 0),))
-    each(SECOND[4:], pass_on)
+    each(SECOND[10:], pass_on)
+    each(FIRST, finish)
+    q_wait_part(2, 1, 0)
+    q_wait_part(2, 1, 1)
+    each(LATE, multiply)
+    each(LATE, pass_on)
 
     down[2].wait_recv()
     down[3].start()
     up[2].wait_recv()
     up[3].start()
-    each(SECOND, finish)
-    q_wait(1, 1)
-    q_wait(2, 1)
     all_pairs(3)
     each(THIRD, pass_on)
-    each(LATE, multiply)
-    each(LATE, pass_on)
+    each(SECOND, finish)
+    each(LATE, finish)
     pairs(((2, 0), (4, 0)))
     each(KEPT, pass_on)
     each(THIRD, finish)
@@ -326,8 +341,8 @@
     up[3].wait_recv()
     all_pairs(4)
     each(LAST, pass_on)
-    for units in (LATE, LAST, KEPT):
-        each(units, finish)
+    each(KEPT, finish)
+    each(LAST, finish)
 
     for c in down + up + q_sends:
         c.wait_send()
@@ -376,7 +391,7 @@
         blocks = pl.pallas_call(
             kernel,
             out_shape=jax.ShapeDtypeStruct((rows, NX * NZ * rows), BF16),
-            in_specs=[pl.BlockSpec(memory_space=pl.ANY)],
+            in_specs=[pl.BlockSpec(memory_space=pltpu.HBM)],
             out_specs=pl.BlockSpec(memory_space=pl.ANY),
             scratch_shapes=[
                 pltpu.VMEM((NQ + NZ - 1, rows, depth), BF16),
@@ -389,7 +404,7 @@
                 pltpu.VMEM((n, *tile), BF16),
                 dma((1,)),
                 dma((NZ,)), dma((NZ,)),
-                dma((7,)), dma((NQ,)),
+                dma((8,)), dma((NQ + 2,)),
                 dma((2 * n,)), dma((2 * n,)),
                 dma((n,)), dma((n,)),
                 dma((n,)), dma((n,)),

time: 87.2 us -> 84 us (0.963)
  Pallas kernels: 82.1 us -> 79.3 us
    pallas_call x1, Pallas kernels: 82.1 us -> 79.3 us  [local(): pl.pallas_call(kernel, out_shape=jax.ShapeDtypeStruct((rows, NX * NZ * ro...]
where the time goes in v3:
time: 84 us; the launch traced here: 82.8 us
  Pallas kernels  79.3 us (94%)
  other arithmetic  2.51 us (3%)
  local copies, waits for them, and re-layouts  1.04 us (1%)
    pallas_call x1, Pallas kernels, local(): pl.pallas_call(kernel, out_shape=jax.ShapeDtypeStruct((rows, NX * NZ * ro...  79.3 us
    convert_element_type x1, other arithmetic, local(): return blocks.astype(F32)  2.51 us

profile of v3, /device:TPU:1, one launch (start us, length us, event | category | flops | bytes accessed | tf_op | source)
XLA Modules:
  0.0 82.8 jit_solution(18285810985661103605)
XLA Ops:
  0.0 0.0 copy-start
  0.0 1.0 %copy-done = bf16[1,256,1024]{2,1,0:T(8,128)(2,1)S(1)} copy-done((bf16[1,256,1024]{2,1,0:T(8,128)(2,1)S(1)}, bf16[1,256,1024]{2,1,0:T(8,128)(2,1)}, u32[]{:S(2)}) %copy-start) | copy-done | bytes 524312
  1.0 79.3 %shard_map.17 = bf16[256,4096]{1,0:T(8,128)(2,1)S(1)} custom-call(bf16[256,1024]{1,0:T(8,128)(2,1)S(1)} %bitcast.1), custom_call_target="tpu_custom_call" | custom-call | tf_op jit(solution)/shard_map/pallas_call | solution.py:391
  80.3 2.5 %convert_element_type.3 = f32[256,4096]{1,0:T(8,128)} convert(bf16[256,4096]{1,0:T(8,128)(2,1)S(1)} %shard_map.17) | non-fusion elementwise | flops 1048576 | bytes 6291456 | tf_op jit(solution)/shard_map/convert_element_type | solution.py:417
Async XLA Ops:
  0.0 1.0 %copy-start = (bf16[1,256,1024]{2,1,0:T(8,128)(2,1)S(1)}, bf16[1,256,1024]{2,1,0:T(8,128)(2,1)}, u32[]{:S(2)}) copy-start(bf16[1,256,1024]{2,1,0:T(8,128)(2,1)} %param.1) | copy-start | bytes 1572868

commit v4 on v3

--- a/solution.py
+++ b/solution.py
@@ -65,7 +65,7 @@
 
     barrier = pltpu.get_barrier_semaphore()
     partners = [other_core, other_lo, other_x, beside, y_up, y_down]
-    partners += [z_off(d) for d in (1, 2, 3, 5, 6, 7)]
+    partners += [z_off(d) for d in range(1, NZ)]
     for who in partners:
         pl.semaphore_signal(barrier, inc=1, device_id=who, device_id_type=MESH)
 
@@ -198,11 +198,15 @@
         e = x_ * ND + d
         return pltpu.make_async_copy(flipped.at[e], b_place(d, x_), b_rsem.at[e])
 
+    def along_z(q):
+        return jnp.logical_or(q == 5, q == 1)
+
     def goes_direct(q, d):
-        return d < ND - 1
+        return jnp.logical_or(d < ND - 1, along_z(q))
 
     def goes_flipped(q, d):
-        return d > 0
+        last = jnp.logical_and(d == ND - 1, along_z(q))
+        return jnp.logical_and(d > 0, jnp.logical_not(last))
 
     def left(yc, d):
         side = jnp.where(yc // 2 == lo, xh, 1 - xh)
@@ -324,6 +328,8 @@
     q_wait_part(2, 1, 1)
     each(LATE, multiply)
     each(LATE, pass_on)
+    pairs(((2, 0), (4, 0)))
+    each(KEPT, pass_on)
 
     down[2].wait_recv()
     down[3].start()
@@ -332,16 +338,14 @@
     all_pairs(3)
     each(THIRD, pass_on)
     each(SECOND, finish)
+    each(THIRD, finish)
     each(LATE, finish)
-    pairs(((2, 0), (4, 0)))
-    each(KEPT, pass_on)
-    each(THIRD, finish)
+    each(KEPT, finish)
 
     down[3].wait_recv()
     up[3].wait_recv()
     all_pairs(4)
     each(LAST, pass_on)
-    each(KEPT, finish)
     each(LAST, finish)
 
     for c in down + up + q_sends:

time: 84 us -> 82.6 us (0.983)
  no operation moved by 1% of the time
where the time goes in v4:
time: 82.6 us; the launch traced here: 82.2 us
  Pallas kernels  78.7 us (95%)
  other arithmetic  2.51 us (3%)
  local copies, waits for them, and re-layouts  1.04 us (1%)
    pallas_call x1, Pallas kernels, local(): pl.pallas_call(kernel, out_shape=jax.ShapeDtypeStruct((rows, NX * NZ * ro...  78.7 us
    convert_element_type x1, other arithmetic, local(): return blocks.astype(F32)  2.51 us

profile of v4, /device:TPU:1, one launch (start us, length us, event | category | flops | bytes accessed | tf_op | source)
XLA Modules:
  0.0 82.2 jit_solution(10564768051755612485)
XLA Ops:
  0.0 0.0 copy-start
  0.0 1.0 %copy-done = bf16[1,256,1024]{2,1,0:T(8,128)(2,1)S(1)} copy-done((bf16[1,256,1024]{2,1,0:T(8,128)(2,1)S(1)}, bf16[1,256,1024]{2,1,0:T(8,128)(2,1)}, u32[]{:S(2)}) %copy-start) | copy-done | bytes 524312
  1.0 78.7 %shard_map.17 = bf16[256,4096]{1,0:T(8,128)(2,1)S(1)} custom-call(bf16[256,1024]{1,0:T(8,128)(2,1)S(1)} %bitcast.1), custom_call_target="tpu_custom_call" | custom-call | tf_op jit(solution)/shard_map/pallas_call | solution.py:395
  79.7 2.5 %convert_element_type.3 = f32[256,4096]{1,0:T(8,128)} convert(bf16[256,4096]{1,0:T(8,128)(2,1)S(1)} %shard_map.17) | non-fusion elementwise | flops 1048576 | bytes 6291456 | tf_op jit(solution)/shard_map/convert_element_type | solution.py:421
Async XLA Ops:
  0.0 1.0 %copy-start = (bf16[1,256,1024]{2,1,0:T(8,128)(2,1)S(1)}, bf16[1,256,1024]{2,1,0:T(8,128)(2,1)}, u32[]{:S(2)}) copy-start(bf16[1,256,1024]{2,1,0:T(8,128)(2,1)} %param.1) | copy-start | bytes 1572868

commit v5 on v4

--- a/solution.py
+++ b/solution.py
@@ -293,6 +293,15 @@
                 @pl.when(q > 0)
                 def _():
                     b_copy(d, xc).start()
+
+    def two(yc, d, body):
+        def step(k, carry):
+            body((yc - y + NY) % NY * 2 + k, d)
+            return carry
+
+        lax.fori_loop(0, NX, step, 0)
+
+    away_rank = (1 - lo) * 2 + core
 
     down[0].wait_recv()
     down[1].start()
@@ -336,17 +345,17 @@
     up[2].wait_recv()
     up[3].start()
     all_pairs(3)
-    each(THIRD, pass_on)
+    two(away_rank, 3, pass_on)
     each(SECOND, finish)
-    each(THIRD, finish)
     each(LATE, finish)
     each(KEPT, finish)
+    two(rank, 3, finish)
 
     down[3].wait_recv()
     up[3].wait_recv()
     all_pairs(4)
-    each(LAST, pass_on)
-    each(LAST, finish)
+    two(away_rank, 4, pass_on)
+    two(rank, 4, finish)
 
     for c in down + up + q_sends:
         c.wait_send()

time: 82.6 us -> 81.8 us (level)
  Pallas kernels: 78.7 us -> 77.2 us
    pallas_call x1, Pallas kernels: 78.7 us -> 77.2 us  [local(): pl.pallas_call(kernel, out_shape=jax.ShapeDtypeStruct((rows, NX * NZ * ro...]
where the time goes in v5:
time: 81.8 us; the launch traced here: 80.8 us
  Pallas kernels  77.2 us (94%)
  other arithmetic  2.51 us (3%)
  local copies, waits for them, and re-layouts  1.04 us (1%)
    pallas_call x1, Pallas kernels, local(): pl.pallas_call(kernel, out_shape=jax.ShapeDtypeStruct((rows, NX * NZ * ro...  77.2 us
    convert_element_type x1, other arithmetic, local(): return blocks.astype(F32)  2.51 us

profile of v5, /device:TPU:1, one launch (start us, length us, event | category | flops | bytes accessed | tf_op | source)
XLA Modules:
  0.0 80.8 jit_solution(11334355574019797984)
XLA Ops:
  0.0 0.0 copy-start
  0.0 1.0 %copy-done = bf16[1,256,1024]{2,1,0:T(8,128)(2,1)S(1)} copy-done((bf16[1,256,1024]{2,1,0:T(8,128)(2,1)S(1)}, bf16[1,256,1024]{2,1,0:T(8,128)(2,1)}, u32[]{:S(2)}) %copy-start) | copy-done | bytes 524312
  1.0 77.2 %shard_map.17 = bf16[256,4096]{1,0:T(8,128)(2,1)S(1)} custom-call(bf16[256,1024]{1,0:T(8,128)(2,1)S(1)} %bitcast.1), custom_call_target="tpu_custom_call" | custom-call | tf_op jit(solution)/shard_map/pallas_call | solution.py:404
  78.3 2.5 %convert_element_type.3 = f32[256,4096]{1,0:T(8,128)} convert(bf16[256,4096]{1,0:T(8,128)(2,1)S(1)} %shard_map.17) | non-fusion elementwise | flops 1048576 | bytes 6291456 | tf_op jit(solution)/shard_map/convert_element_type | solution.py:430
Async XLA Ops:
  0.0 1.0 %copy-start = (bf16[1,256,1024]{2,1,0:T(8,128)(2,1)S(1)}, bf16[1,256,1024]{2,1,0:T(8,128)(2,1)}, u32[]{:S(2)}) copy-start(bf16[1,256,1024]{2,1,0:T(8,128)(2,1)} %param.1) | copy-start | bytes 1572868

commit v6 on v5

--- a/solution.py
+++ b/solution.py
@@ -243,12 +243,12 @@
     def pairs(todo):
         each(todo, lambda q, d: multiply_both((y + q // 2) % NY, d))
 
-    def all_pairs(d):
+    def all_pairs(d, first, last):
         def step(k, carry):
             multiply_both(((k // 2 + 1 + lo) % 2) * 2 + k % 2, d)
             return carry
 
-        lax.fori_loop(0, NY, step, 0)
+        lax.fori_loop(first, last, step, 0)
 
     def pass_on(q, d):
         yc, xc = block(q)
@@ -344,8 +344,9 @@
     down[3].start()
     up[2].wait_recv()
     up[3].start()
-    all_pairs(3)
+    all_pairs(3, 0, 3)
     two(away_rank, 3, pass_on)
+    all_pairs(3, 3, NY)
     each(SECOND, finish)
     each(LATE, finish)
     each(KEPT, finish)
@@ -353,8 +354,9 @@
 
     down[3].wait_recv()
     up[3].wait_recv()
-    all_pairs(4)
+    all_pairs(4, 0, 3)
     two(away_rank, 4, pass_on)
+    all_pairs(4, 3, NY)
     two(rank, 4, finish)
 
     for c in down + up + q_sends:

time: 81.8 us -> 81.8 us (level)
  no operation moved by 1% of the time
where the time goes in v6:
time: 81.8 us; the launch traced here: 80.2 us
  Pallas kernels  76.7 us (94%)
  other arithmetic  2.51 us (3%)
  local copies, waits for them, and re-layouts  1.04 us (1%)
    pallas_call x1, Pallas kernels, local(): pl.pallas_call(kernel, out_shape=jax.ShapeDtypeStruct((rows, NX * NZ * ro...  76.7 us
    convert_element_type x1, other arithmetic, local(): return blocks.astype(F32)  2.51 us

profile of v6, /device:TPU:1, one launch (start us, length us, event | category | flops | bytes accessed | tf_op | source)
XLA Modules:
  0.0 80.2 jit_solution(14951689411647931395)
XLA Ops:
  0.0 0.0 copy-start
  0.0 1.0 %copy-done = bf16[1,256,1024]{2,1,0:T(8,128)(2,1)S(1)} copy-done((bf16[1,256,1024]{2,1,0:T(8,128)(2,1)S(1)}, bf16[1,256,1024]{2,1,0:T(8,128)(2,1)}, u32[]{:S(2)}) %copy-start) | copy-done | bytes 524312
  1.0 76.7 %shard_map.17 = bf16[256,4096]{1,0:T(8,128)(2,1)S(1)} custom-call(bf16[256,1024]{1,0:T(8,128)(2,1)S(1)} %bitcast.1), custom_call_target="tpu_custom_call" | custom-call | tf_op jit(solution)/shard_map/pallas_call | solution.py:406
  77.7 2.5 %convert_element_type.3 = f32[256,4096]{1,0:T(8,128)} convert(bf16[256,4096]{1,0:T(8,128)(2,1)S(1)} %shard_map.17) | non-fusion elementwise | flops 1048576 | bytes 6291456 | tf_op jit(solution)/shard_map/convert_element_type | solution.py:432
Async XLA Ops:
  0.0 1.0 %copy-start = (bf16[1,256,1024]{2,1,0:T(8,128)(2,1)S(1)}, bf16[1,256,1024]{2,1,0:T(8,128)(2,1)}, u32[]{:S(2)}) copy-start(bf16[1,256,1024]{2,1,0:T(8,128)(2,1)} %param.1) | copy-start | bytes 1572868
